TPU v7x, 512 devices: a whole 4x8x8 slice. The times are simulated.
512 devices in a mesh: dp: 8 (over z_lo, x), fsdp: 16 (over y, core), tensor: 4 (over z_hi).
Axes of the slice: x: 4, y: 8, z: 8 (z_hi: 4, z_lo: 2; z = z_hi * 2 + z_lo), core: 2. Of those that a mesh axis runs over, the one named last changes fastest.
Arguments:
- activations: bfloat16 [8192, 16384], P(('dp', 'fsdp', 'tensor')), may hold values from -6 to 6
- cotangent: bfloat16 [8192, 8192], P(('dp', 'fsdp'), 'tensor'), may hold values from -6 to 6
- left_root: bfloat16 [16, 8, 1024, 1024], P('fsdp', 'tensor', 'dp'), may hold values from -1 to 3
- right_root: bfloat16 [16, 8, 1024, 1024], P('fsdp', 'tensor', 'dp'), may hold values from -1 to 3
Outputs:
- left_stat: float32 [16, 8, 1024, 1024], P('fsdp', 'tensor', 'dp')
- right_stat: float32 [16, 8, 1024, 1024], P('fsdp', 'tensor', 'dp')
- update: bfloat16 [16, 8, 1024, 1024], P('fsdp', 'tensor', 'dp')
All inputs are finite; a program needn't handle non-finite values.
Results may differ from a plain program's by a relative error of at most 0.02.
Values may be sent and summed in bfloat16 or wider, within the bound.
A program may use at most 64 MiB of HBM per device.

v0:
```python
import jax
import jax.numpy as jnp
from jax import lax
from jax.sharding import PartitionSpec as P


def on_device(activations, cotangent, left_root, right_root):
    dp_count = lax.axis_size("dp")
    fsdp_count = lax.axis_size("fsdp")
    tok_dev = cotangent.shape[0]
    factor = float(tok_dev * dp_count * fsdp_count) ** (-0.5)
    gathered = lax.all_gather(activations, "tensor", axis=0, tiled=True)
    token_rows = lax.all_to_all(gathered, "fsdp", split_axis=1, concat_axis=0, tiled=True)
    selected = token_rows
    partial_value = lax.dot_general(
        selected,
        lax.all_gather(cotangent, "fsdp", axis=0, tiled=True),
        (((0,), (0,)), ((), ())),
        preferred_element_type=jnp.float32,
    )
    partial_value = partial_value * factor
    row_blocks = left_root.shape[0]
    col_blocks = left_root.shape[1]
    share = left_root.shape[2]
    block = left_root.shape[3]
    shaped = partial_value.reshape(row_blocks, block, col_blocks * block)
    own_index = lax.axis_index("dp")
    local_rows = lax.psum_scatter(
        shaped.astype(jnp.bfloat16), "dp", scatter_dimension=1, tiled=True
    )
    local_blocks = local_rows.reshape(row_blocks, share, col_blocks, block)
    portion = lax.all_gather(local_rows, "dp", axis=1, tiled=True)
    length = portion.shape[1]
    blocks = portion.reshape(row_blocks, length, col_blocks, block)
    own_columns = lax.dynamic_slice_in_dim(blocks, own_index * share, share, 3)
    left_piece = jnp.einsum(
        "rsck,rnck->rcsn", local_blocks, blocks, preferred_element_type=jnp.float32
    )
    left_stat = left_piece
    right_stat = jnp.einsum(
        "rnck,rncj->rckj", own_columns, blocks, preferred_element_type=jnp.float32
    )
    lifted = jnp.einsum("rcsn,rncj->rcsj", left_root, blocks, preferred_element_type=jnp.float32)
    left_stat, right_stat, lifted = (left_stat, right_stat, lifted)
    lifted_low = lifted.astype(jnp.bfloat16)
    portion = lax.all_gather(right_root, "dp", axis=2, tiled=True)
    selected = lifted_low
    update = jnp.einsum("rcsn,rcnj->rcsj", selected, portion, preferred_element_type=jnp.float32)
    inverse_block = 1.0 / block
    return (left_stat * inverse_block, right_stat * inverse_block, update.astype(jnp.bfloat16))


def solution(mesh):
    return jax.shard_map(
        on_device,
        mesh=mesh,
        in_specs=(
            P(("dp", "fsdp", "tensor"), None),
            P(("dp", "fsdp"), "tensor"),
            P("fsdp", "tensor", "dp", None),
            P("fsdp", "tensor", "dp", None),
        ),
        out_specs=(
            P("fsdp", "tensor", "dp", None),
            P("fsdp", "tensor", "dp", None),
            P("fsdp", "tensor", "dp", None),
        ),
        check_vma=False,
    )
```

profile of v0, /device:TPU:1, one launch (start us, length us, event | category | flops | bytes accessed | tf_op | source)
XLA Modules:
  0.0 343.4 jit_solution(14228610453964859098)
XLA Ops:
  7.2 0.0 copy-start
  7.2 0.0 all-gather.5.cloned.1.call-start
  7.2 0.7 all-gather.5.cloned.1.call-update
  7.9 0.0 all-gather.7.cloned.1.call-start
  8.0 0.7 all-gather.7.cloned.1.call-update
  8.7 0.0 reduce-scatter.2.cloned.1.call-start
  8.7 60.5 %all-gather.5.cloned.1.call-done = bf16[64,16384]{1,0:T(8,128)(2,1)} async-done(((bf16[16,16384]{1,0:T(8,128)(2,1)}), bf16[64,16384]{1,0:T(8,128)(2,1)}) %all-gather.5.cloned.1.call-update) | async-done | bytes 2097168 | tf_op jit(solution)/shard_map/all_gather | solution.py:12
  69.2 1.8 copy.35
  71.0 75.4 %all_to_all.19 = bf16[64,16,1024]{2,0,1:T(8,128)(2,1)S(1)} all-to-all(bf16[64,16,1024]{2,0,1:T(8,128)(2,1)S(1)} %bitcast.38), channel_id=1, replica_groups=mesh['dp'=8,'fsdp'=16,'tensor'=4] {'fsdp'}, dimensions={1} | all-to-all | bytes 4194304 | tf_op jit(solution)/shard_map/all_to_all | solution.py:13
  146.4 1.6 all-gather.7.cloned.1.call-done
  148.0 8.3 %fusion.2 = bf16[1,1024,2048]{2,1,0:T(8,128)(2,1)} fusion(bf16[1024,1024]{1,0:T(8,128)(2,1)S(1)} %bitcast.40, bf16[1024,2048]{1,0:T(8,128)(2,1)} %all-gather.7.cloned.1.call-done), kind=kOutput, calls=%fused_computation.3 | convolution fusion | flops 4299161600 | bytes 10485760 | tf_op jit(solution)/shard_map/dot_general | solution.py:15
  156.4 0.0 reduce-scatter.2.cloned.1.call-update
  156.4 0.0 all-gather.9.cloned.1.call-start
  156.4 56.9 %reduce-scatter.2.cloned.1.call-done = bf16[1,128,2048]{2,1,0:T(8,128)(2,1)} async-done(((bf16[1,1024,2048]{2,1,0:T(8,128)(2,1)}), bf16[1,128,2048]{2,1,0:T(8,128)(2,1)}) %reduce-scatter.2.cloned.1.call-update) | async-done | bytes 524304 | tf_op jit(solution)/shard_map/reduce_scatter | solution.py:28
  213.4 0.0 all-gather.9.cloned.1.call-update
  213.4 0.0 all-gather.11.cloned.1.call-start
  213.4 0.5 all-gather.11.cloned.1.call-update
  214.0 1.4 reshape.46
  215.4 56.6 %all-gather.9.cloned.1.call-done = bf16[1,1024,2048]{2,1,0:T(8,128)(2,1)} async-done(((bf16[1,128,2048]{2,1,0:T(8,128)(2,1)}), bf16[1,1024,2048]{2,1,0:T(8,128)(2,1)}) %all-gather.9.cloned.1.call-update) | async-done | bytes 4194320 | tf_op jit(solution)/shard_map/all_gather | solution.py:32
  272.1 7.8 %reshape.48 = bf16[1,1024,2,1024]{3,2,1,0:T(2,128)(2,1)} reshape(bf16[1,1024,2048]{2,1,0:T(8,128)(2,1)} %all-gather.9.cloned.1.call-done) | data formatting | bytes 8388608 | tf_op jit(solution)/shard_map/reshape | solution.py:34
  279.9 1.4 constant_dynamic-slice_fusion
  281.3 0.4 copy.25
  281.7 6.3 %copy.30 = bf16[1,1024,2048]{1,2,0:T(8,128)(2,1)} copy(bf16[1,1024,2048]{2,1,0:T(8,128)(2,1)} %all-gather.9.cloned.1.call-done) | data formatting | bytes 8388608 | tf_op jit(solution)/shard_map/reshape.1
  288.0 0.0 copy-start.1
  288.0 4.8 %fusion.3 = f32[1,2,128,1024]{3,2,1,0:T(8,128)} fusion(bf16[1024,2,1024]{0,2,1:T(8,128)(2,1)} %bitcast.35, bf16[1,1024,2,128]{1,3,2,0:T(8,128)(2,1)S(1)} %copy.25), kind=kOutput, calls=%fused_computation.6 | convolution fusion | flops 537133056 | bytes 5767168 | tf_op jit(solution)/shard_map/rnck,rncj->rckj/dot_general | solution.py:40
  292.9 0.0 copy-done.1
  292.9 1.8 fusion.4
  294.6 36.2 %all-gather.11.cloned.1.call-done = bf16[1,2,1024,1024]{3,2,1,0:T(8,128)(2,1)} async-done(((bf16[1,2,128,1024]{3,2,1,0:T(8,128)(2,1)}), bf16[1,2,1024,1024]{3,2,1,0:T(8,128)(2,1)}) %all-gather.11.cloned.1.call-update) | async-done | bytes 4194320 | tf_op jit(solution)/shard_map/all_gather | solution.py:46
  330.8 0.0 copy-done
  330.8 6.1 %fusion.8 = bf16[1,2,128,1024]{3,2,1,0:T(8,128)(2,1)} fusion(bf16[1,2,1024,1024]{3,2,1,0:T(8,128)(2,1)} %all-gather.11.cloned.1.call-done, bf16[1024,2,1024]{0,2,1:T(8,128)(2,1)} %bitcast.36, bf16[1,2,128,1024]{3,2,1,0:T(8,128)(2,1)S(1)} %copy-done), kind=kOutput, calls=%fused_computation.11 | convolution fusion | flops 1074266112 | bytes 9437184 | tf_op jit(solution)/shard_map/rcsn,rcnj->rcsj/dot_general | solution.py:48
Async XLA Ops:
  7.2 323.6 %copy-start = (bf16[1,2,128,1024]{3,2,1,0:T(8,128)(2,1)S(1)}, bf16[1,2,128,1024]{3,2,1,0:T(8,128)(2,1)}, u32[]{:S(2)}) copy-start(bf16[1,2,128,1024]{3,2,1,0:T(8,128)(2,1)} %param.6) | copy-start | bytes 1572868
  7.2 62.1 %all-gather.5.cloned.1.call-start = ((), (), s32[]{:S(2)}) async-start(), calls=%async_computation.2 | async-start | bytes 2621440 | tf_op jit(solution)/shard_map/all_gather | solution.py:12
  7.9 140.1 %all-gather.7.cloned.1.call-start = ((), (), s32[]{:S(2)}) async-start(), calls=%async_computation.3 | async-start | bytes 4456448 | tf_op jit(solution)/shard_map/all_gather | solution.py:17
  8.7 204.7 %reduce-scatter.2.cloned.1.call-start = ((), (), s32[]{:S(2)}) async-start(), calls=%async_computation.4 | async-start | bytes 4718592 | tf_op jit(solution)/shard_map/reduce_scatter | solution.py:28
  156.4 115.7 %all-gather.9.cloned.1.call-start = ((), (), s32[]{:S(2)}) async-start(), calls=%async_computation.5 | async-start | bytes 4718592 | tf_op jit(solution)/shard_map/all_gather | solution.py:32
  213.4 117.4 %all-gather.11.cloned.1.call-start = ((), (), s32[]{:S(2)}) async-start(), calls=%async_computation.6 | async-start | bytes 4718592 | tf_op jit(solution)/shard_map/all_gather | solution.py:46
  288.0 4.8 %copy-start.1 = (bf16[1,1024,2048]{1,2,0:T(8,128)(2,1)S(1)}, bf16[1,1024,2048]{1,2,0:T(8,128)(2,1)}, u32[]{:S(2)}) copy-start(bf16[1,1024,2048]{1,2,0:T(8,128)(2,1)} %copy.30) | copy-start | bytes 12582916
Sparse Core Ops, SparseCore 0:
  10.1 59.0 all-gather.4
  71.4 76.6 all-gather.6
  156.5 56.8 reduce-scatter.1
  215.3 56.7 all-gather.8
  274.0 56.7 all-gather.10
where the time goes:
time: 344 us; the launch traced here: 343 us
  waiting for transfers between devices  214 us (62%)
  blocking collectives  75.4 us (22%)
  matrix products  21 us (6%)
  local copies, waits for them, and re-layouts  19.2 us (6%)
  between operations  13.8 us (4%)
    all_to_all x1, blocking collectives, on_device(): lax.all_to_all(gathered, 'fsdp', split_axis=1, concat_axis=0, tiled=True)  75.4 us
    all_gather x1, waiting for transfers between devices, on_device(): gathered = lax.all_gather(activations, 'tensor', axis=0, tiled=True)  60.5 us
    reduce_scatter x1, waiting for transfers between devices, on_device(): lax.psum_scatter(shaped.astype(jnp.bfloat16), 'dp', scatter_dimension=1,...  56.9 us
    all_gather x1, waiting for transfers between devices, on_device(): portion = lax.all_gather(local_rows, 'dp', axis=1, tiled=True)  56.6 us
    all_gather x1, waiting for transfers between devices, on_device(): portion = lax.all_gather(right_root, 'dp', axis=2, tiled=True)  36.2 us
    dot_general x1, matrix products, on_device(): lax.dot_general(selected, lax.all_gather(cotangent, 'fsdp', axis=0, tiled...  8.34 us
    reshape x1, local copies, waits for them, and re-layouts, on_device(): blocks = portion.reshape(row_blocks, length, col_blocks, block)  7.82 us
  transfers between devices with their start and end apart: 5, of which 5 were waited for; matrix products, arithmetic and copies ran while one was open for 7% of the time, Pallas kernels for 0%

commit v1 on v0

v1 whole, which is shorter than its diff:
```python
import functools

import jax
import jax.numpy as jnp
from jax import lax
from jax.experimental import pallas as pl
from jax.experimental.pallas import tpu as pltpu
from jax.sharding import PartitionSpec as P

MESH = pl.DeviceIdType.MESH
X, Y, Z, CORES = 4, 8, 8, 2
F = Y * CORES
T = Z // 2
PIECE = 128
BLOCK = 1024
ROWS = 16
SLOT = F * ROWS
TILE = 256


def mod(value, size):
    return lax.rem(value + 2 * size, size)


def scaled(index, size):
    return pl.multiple_of(index * size, size)


def kernel(
    factor,
    a_ref, c_ref, lr_ref, rr_ref,
    left_ref, right_ref, upd_ref,
    a_buf, c_buf, g_buf, r_buf, l_buf, at_buf, t_buf, relay, near, gt_buf, lift_buf, o_buf,
    local_sem, swap_send, swap_recv,
    a_send, a_recv, c_send, c_recv, sib_send, sib_recv,
    z_send, z_recv, t_send, t_recv, g_send, g_recv, r_send, r_recv, o_send, o_recv,
):
    m = lax.axis_index("dp")
    f = lax.axis_index("fsdp")
    t = lax.axis_index("tensor")
    zl, x = lax.div(m, X), lax.rem(m, X)
    y, core = lax.div(f, CORES), lax.rem(f, CORES)
    z = 2 * t + zl
    other = 1 - zl

    def on_x(step):
        return (zl * X + mod(x + step, X), f, t)

    def on_y(step):
        return (m, mod(y + step, Y) * CORES + core, t)

    def on_z(step):
        there = mod(z + step, Z)
        return (lax.rem(there, 2) * X + x, f, lax.div(there, 2))

    def slot_of(there):
        return lax.rem(there, 2) * T + lax.div(there, 2)

    sibling = (m, y * CORES + 1 - core, t)
    partner = (other * X + x, f, t)
    sign = (1, -1)

    started = []

    def put(src, dst, send, recv, device):
        copy = pltpu.make_async_remote_copy(
            src_ref=src, dst_ref=dst, send_sem=send, recv_sem=recv,
            device_id=device, device_id_type=MESH,
        )
        copy.start()
        started.append(copy)

    def arrived(dst, recv):
        pltpu.make_async_remote_copy(
            src_ref=dst, dst_ref=dst, send_sem=recv, recv_sem=recv,
            device_id=sibling, device_id_type=MESH,
        ).wait_recv()

    barrier = pltpu.get_barrier_semaphore()

    def greet(d, carry):
        pl.semaphore_signal(barrier, inc=1, device_id=(m, mod(f + d, F), t), device_id_type=MESH)
        return carry

    lax.fori_loop(1, F, greet, 0)
    for device in (on_x(1), on_x(-1), on_z(1), on_z(-1)):
        pl.semaphore_signal(barrier, inc=1, device_id=device, device_id_type=MESH)

    slot = slot_of(z)
    my_rows = scaled(f, ROWS)
    local = [
        pltpu.make_async_copy(
            a_ref.at[:, pl.ds(scaled(f, BLOCK), BLOCK)],
            a_buf.at[slot, pl.ds(my_rows, ROWS), :], local_sem.at[0]),
        pltpu.make_async_copy(
            c_ref.at[:, :, pl.ds(scaled(zl, BLOCK), BLOCK)],
            c_buf.at[pl.ds(zl * T, T), pl.ds(my_rows, ROWS), :], local_sem.at[1]),
        pltpu.make_async_copy(lr_ref.at[zl], l_buf.at[zl], local_sem.at[2]),
        pltpu.make_async_copy(rr_ref.at[zl], r_buf.at[zl, x], local_sem.at[3]),
    ]
    for copy in local:
        copy.start()
    pl.semaphore_wait(barrier, F - 1 + 4)

    def c_chunk(half, owner):
        return c_buf.at[pl.ds(half * T, T), pl.ds(scaled(owner, ROWS), ROWS), :]

    put(c_ref.at[:, :, pl.ds(scaled(other, BLOCK), BLOCK)], c_chunk(zl, f),
        swap_send.at[0], swap_recv.at[0], partner)

    def a_copy(d):
        to = mod(f + d, F)
        return pltpu.make_async_remote_copy(
            src_ref=a_ref.at[:, pl.ds(scaled(to, BLOCK), BLOCK)],
            dst_ref=a_buf.at[slot, pl.ds(my_rows, ROWS), :],
            send_sem=a_send.at[d], recv_sem=a_recv.at[d],
            device_id=(m, to, t), device_id_type=MESH)

    def a_start(d, carry):
        a_copy(d).start()
        return carry

    lax.fori_loop(1, F, a_start, 0)

    def c_share(src, half, owner, way, step):
        put(src, c_chunk(half, owner), sib_send.at[half, way, step], sib_recv.at[half, way, step], sibling)

    def c_first(src, half):
        for way in (0, 1):
            put(src, c_chunk(half, f), c_send.at[way, half, 0], c_recv.at[way, half, 1], on_y(sign[way]))
        c_share(src, half, f, 0, 0)

    def r_first(src, half):
        for way in (0, 1):
            put(src, r_buf.at[half, x], r_send.at[way, half, 0], r_recv.at[way, half, 1], on_x(sign[way]))

    c_first(c_ref.at[:, :, pl.ds(scaled(zl, BLOCK), BLOCK)], zl)
    r_first(rr_ref.at[zl], zl)
    put(rr_ref.at[other], r_buf.at[zl, x], swap_send.at[1], swap_recv.at[1], partner)
    put(lr_ref.at[other], l_buf.at[zl], swap_send.at[2], swap_recv.at[2], partner)
    arrived(c_chunk(other, f), swap_recv.at[0])
    c_first(c_chunk(other, f), other)

    def a_wait(d, carry):
        arrived(a_buf.at[slot, pl.ds(scaled(mod(f - d, F), ROWS), ROWS), :], a_recv.at[d])
        return carry

    local[0].wait()
    lax.fori_loop(1, F, a_wait, 0)

    target = (mod(x + 2, X), mod(x + 1, X), mod(x - 1, X), x)

    def lanes(part, half):
        return pl.ds(pl.multiple_of((half * X + target[part]) * PIECE, PIECE), PIECE)

    def z_put(part, half, way, step, owner):
        ref = a_buf.at[owner, :, lanes(part, half)]
        put(ref, ref, z_send.at[way, part, half, step], z_recv.at[way, part, half, step + 1], on_z(sign[way]))

    def z_first(part):
        for half in (0, 1):
            for way in (0, 1):
                z_put(part, half, way, 0, slot)

    def z_event(part, step):
        for half in (0, 1):
            for way in (0, 1):
                if step == Z // 2 and way != half:
                    continue
                owner = slot_of(mod(z - sign[way] * step, Z))
                arrived(a_buf.at[owner, :, lanes(part, half)], z_recv.at[way, part, half, step])
                if step < Z // 2 - 1 or (step == Z // 2 - 1 and way == half):
                    z_put(part, half, way, step, owner)

    def c_event(step):
        for half in (0, 1):
            for way in (0, 1):
                if step == Y // 2 and way != half:
                    continue
                owner = mod(y - sign[way] * step, Y) * CORES + core
                chunk = c_chunk(half, owner)
                arrived(chunk, c_recv.at[way, half, step])
                if step < Y // 2 - 1 or (step == Y // 2 - 1 and way == half):
                    put(chunk, chunk, c_send.at[way, half, step], c_recv.at[way, half, step + 1],
                        on_y(sign[way]))
                c_share(chunk, half, owner, way, step)

    def c_rest():
        for step in range(Y // 2 + 1):
            for half in (0, 1):
                for way in (0, 1):
                    if (step == Y // 2 and way != half) or (step == 0 and way == 1):
                        continue
                    owner = mod(y - sign[way] * step, Y) * CORES + 1 - core
                    arrived(c_chunk(half, owner), sib_recv.at[half, way, step])

    def x_ring(ref_of, send, recv, step):
        for half in (0, 1):
            for way in (0, 1):
                if step == X // 2 and way != half:
                    continue
                ref = ref_of(half, mod(x - sign[way] * step, X))
                arrived(ref, recv.at[way, half, step])
                if step < X // 2 - 1 or (step == X // 2 - 1 and way == half):
                    put(ref, ref, send.at[way, half, step], recv.at[way, half, step + 1], on_x(sign[way]))

    def r_chunk(half, owner):
        return r_buf.at[half, owner]

    def g_chunk(half, owner):
        return g_buf.at[pl.ds(pl.multiple_of((half * X + owner) * PIECE, PIECE), PIECE), :]

    def transpose(part):
        for half in (0, 1):
            for k in range(Z):
                at_buf[pl.ds(half * PIECE, PIECE), pl.ds(k * SLOT, SLOT)] = a_buf[k, :, lanes(part, half)].T

    def columns(n):
        return pl.ds(pl.multiple_of(n * TILE, TILE), TILE)

    def term_tile(part, n):
        cols = columns(n)
        value = jnp.dot(
            at_buf[...], c_buf[:, :, cols].reshape(Z * SLOT, TILE),
            preferred_element_type=jnp.float32,
        ) * factor
        upper, lower = value[:PIECE], value[PIECE:]
        if part == 1:
            upper = upper + relay[0, :, cols].astype(jnp.float32)
        if part == 2:
            lower = lower + relay[1, :, cols].astype(jnp.float32)
        if part == 3:
            upper = upper + near[0, 0, :, cols].astype(jnp.float32) + near[1, 0, :, cols].astype(jnp.float32)
            lower = lower + near[0, 1, :, cols].astype(jnp.float32) + near[1, 1, :, cols].astype(jnp.float32)
            g_chunk(0, x)[:, cols] = upper.astype(jnp.bfloat16)
            g_chunk(1, x)[:, cols] = lower.astype(jnp.bfloat16)
        else:
            t_buf[part, 0, :, cols] = upper.astype(jnp.bfloat16)
            t_buf[part, 1, :, cols] = lower.astype(jnp.bfloat16)

    def term_tiles(part, first, last):
        def body(n, carry):
            term_tile(part, n)
            return carry
        lax.fori_loop(first, last, body, 0)

    def x_before(part):
        if part == 1:
            arrived(relay.at[0], t_recv.at[0])
        if part == 2:
            arrived(relay.at[1], t_recv.at[1])
        if part == 3:
            arrived(near.at[0], t_recv.at[2])
            arrived(near.at[1], t_recv.at[3])

    def x_after(part):
        if part == 0:
            put(t_buf.at[0, 0], relay.at[0], t_send.at[0], t_recv.at[0], on_x(1))
            put(t_buf.at[0, 1], relay.at[1], t_send.at[1], t_recv.at[1], on_x(-1))
        if part == 1:
            put(t_buf.at[1], near.at[0], t_send.at[2], t_recv.at[2], on_x(1))
        if part == 2:
            put(t_buf.at[2], near.at[1], t_send.at[3], t_recv.at[3], on_x(-1))
        if part == 3:
            for half in (0, 1):
                for way in (0, 1):
                    put(g_chunk(half, x), g_chunk(half, x), g_send.at[way, half, 0],
                        g_recv.at[way, half, 1], on_x(sign[way]))

    z_first(0)
    z_first(1)
    arrived(r_chunk(other, x), swap_recv.at[1])
    r_first(r_chunk(other, x), other)
    z_event(0, 1)
    c_event(1)
    z_event(0, 2)
    c_event(2)
    z_event(0, 3)
    x_ring(r_chunk, r_send, r_recv, 1)
    c_event(3)
    z_event(0, 4)
    c_event(4)
    local[1].wait()
    c_rest()
    for part in range(4):
        if part < 2:
            z_first(part + 2)
        transpose(part)
        if part < 3:
            z_event(part + 1, 1)
        x_before(part)
        term_tiles(part, 0, 2)
        if part < 3:
            z_event(part + 1, 2)
        term_tiles(part, 2, 4)
        x_after(part)
        if part < 3:
            z_event(part + 1, 3)
            z_event(part + 1, 4)

    x_ring(g_chunk, g_send, g_recv, 1)
    local[2].wait()
    local[3].wait()
    arrived(l_buf.at[other], swap_recv.at[2])
    x_ring(r_chunk, r_send, r_recv, 2)
    x_ring(g_chunk, g_send, g_recv, 2)

    def own_rows(half):
        return g_chunk(half, x)[...]

    def own_lanes(half):
        return pl.ds(pl.multiple_of((half * X + x) * PIECE, PIECE), PIECE)

    for half in (0, 1):
        gt_buf[pl.ds(half * PIECE, PIECE), :] = g_buf[:, own_lanes(half)].T

    def keep(which, cols, value):
        value = value.astype(jnp.bfloat16)
        o_buf[which, 0, :, cols] = value[:PIECE]
        o_buf[which, 1, :, cols] = value[PIECE:]

    outs = (left_ref, right_ref, upd_ref)
    inverse = 1.0 / BLOCK

    def ship(which):
        put(o_buf.at[which, other], outs[which].at[zl], o_send.at[which], o_recv.at[which], partner)
        copy = pltpu.make_async_copy(o_buf.at[which, zl], outs[which].at[zl], local_sem.at[4 + which])
        copy.start()
        return copy

    def left_tile(n, carry):
        rows = jnp.concatenate([own_rows(0), own_rows(1)], axis=0)
        keep(0, columns(n), inverse * lax.dot_general(
            rows, g_buf[columns(n), :], (((1,), (1,)), ((), ())),
            preferred_element_type=jnp.float32))
        return carry

    def right_tile(n, carry):
        keep(1, columns(n), inverse * jnp.dot(
            gt_buf[...], g_buf[:, columns(n)], preferred_element_type=jnp.float32))
        return carry

    def lift_tile(n, carry):
        rows = l_buf[...].reshape(2 * PIECE, BLOCK)
        lift_buf[:, columns(n)] = jnp.dot(
            rows, g_buf[:, columns(n)], preferred_element_type=jnp.float32).astype(jnp.bfloat16)
        return carry

    def upd_tile(n, carry):
        keep(2, columns(n), jnp.dot(
            lift_buf[...], r_buf[:, :, :, columns(n)].reshape(BLOCK, TILE),
            preferred_element_type=jnp.float32))
        return carry

    tiles = BLOCK // TILE
    lax.fori_loop(0, tiles, left_tile, 0)
    kept = [ship(0)]
    lax.fori_loop(0, tiles, right_tile, 0)
    kept.append(ship(1))
    lax.fori_loop(0, tiles, lift_tile, 0)
    lax.fori_loop(0, tiles, upd_tile, 0)
    kept.append(ship(2))

    def a_drain(d, carry):
        a_copy(d).wait_send()
        return carry

    lax.fori_loop(1, F, a_drain, 0)
    for copy in started:
        copy.wait_send()
    for copy in kept:
        copy.wait()
    for which in range(3):
        arrived(outs[which].at[other], o_recv.at[which])


def on_device(activations, cotangent, left_root, right_root):
    tokens = cotangent.shape[0]
    factor = float(tokens * lax.axis_size("dp") * lax.axis_size("fsdp")) ** (-0.5)
    bf16 = jnp.bfloat16
    dma = pltpu.SemaphoreType.DMA
    anywhere = pl.BlockSpec(memory_space=pl.ANY)
    piece = jax.ShapeDtypeStruct((2, PIECE, BLOCK), bf16)
    left, right, update = pl.pallas_call(
        functools.partial(kernel, factor),
        out_shape=(piece, piece, piece),
        in_specs=[anywhere] * 4,
        out_specs=(anywhere,) * 3,
        scratch_shapes=[
            pltpu.VMEM((Z, SLOT, BLOCK), bf16),
            pltpu.VMEM((Z, SLOT, BLOCK), bf16),
            pltpu.VMEM((BLOCK, BLOCK), bf16),
            pltpu.VMEM((2, X, PIECE, BLOCK), bf16),
            pltpu.VMEM((2, PIECE, BLOCK), bf16),
            pltpu.VMEM((2 * PIECE, Z * SLOT), bf16),
            pltpu.VMEM((3, 2, PIECE, BLOCK), bf16),
            pltpu.VMEM((2, PIECE, BLOCK), bf16),
            pltpu.VMEM((2, 2, PIECE, BLOCK), bf16),
            pltpu.VMEM((2 * PIECE, BLOCK), bf16),
            pltpu.VMEM((2 * PIECE, BLOCK), bf16),
            pltpu.VMEM((3, 2, PIECE, BLOCK), bf16),
            dma((7,)), dma((3,)), dma((3,)),
            dma((F,)), dma((F,)),
            dma((2, 2, 5)), dma((2, 2, 5)), dma((2, 2, 5)), dma((2, 2, 5)),
            dma((2, 4, 2, 5)), dma((2, 4, 2, 5)),
            dma((4,)), dma((4,)),
            dma((2, 2, 3)), dma((2, 2, 3)),
            dma((2, 2, 3)), dma((2, 2, 3)),
            dma((3,)), dma((3,)),
        ],
        compiler_params=pltpu.CompilerParams(
            collective_id=0, has_side_effects=True, vmem_limit_bytes=48 * 1024 * 1024
        ),
        cost_estimate=pl.CostEstimate(
            flops=6 * 2**30, bytes_accessed=8 * 2**20, transcendentals=0),
    )(
        activations,
        cotangent.reshape(T, ROWS, 2 * BLOCK),
        left_root.reshape(2, PIECE, BLOCK),
        right_root.reshape(2, PIECE, BLOCK),
    )
    shape = left_root.shape
    return (
        left.reshape(shape).astype(jnp.float32),
        right.reshape(shape).astype(jnp.float32),
        update.reshape(shape),
    )


def solution(mesh):
    return jax.shard_map(
        on_device,
        mesh=mesh,
        in_specs=(
            P(("dp", "fsdp", "tensor"), None),
            P(("dp", "fsdp"), "tensor"),
            P("fsdp", "tensor", "dp", None),
            P("fsdp", "tensor", "dp", None),
        ),
        out_specs=(
            P("fsdp", "tensor", "dp", None),
            P("fsdp", "tensor", "dp", None),
            P("fsdp", "tensor", "dp", None),
        ),
        check_vma=False,
    )
```

time: 344 us -> 144 us (0.42)
  the two profiles are of different devices: /device:TPU:1 before, /device:TPU:2 now
where the time goes in v1:
time: 144 us
  Pallas kernels  137 us (95%)
  local copies, waits for them, and re-layouts  4.86 us (3%)
  other arithmetic  1.56 us (1%)
    pallas_call x1, Pallas kernels, on_device(): pl.pallas_call(functools.partial(kernel, factor), out_shape=(piece, piece...  137 us
    unnamed x9, local copies, waits for them, and re-layouts  4.86 us

profile of v1, /device:TPU:2, one launch (start us, length us, event | category | flops | bytes accessed | tf_op | source)
XLA Modules:
  0.0 144.2 jit_solution(3002240764493366533)
XLA Ops:
  0.6 0.0 copy-start
  0.6 1.0 copy-done
  1.7 0.0 copy-start.1
  1.7 1.0 copy-done.1
  2.7 0.0 copy-start.2
  2.7 1.0 copy-done.2
  3.8 0.0 copy-start.3
  3.8 0.9 copy-done.3
  4.7 137.1 %shard_map.67 = (bf16[2,128,1024]{2,1,0:T(8,128)(2,1)S(1)}, bf16[2,128,1024]{2,1,0:T(8,128)(2,1)S(1)}, bf16[2,128,1024]{2,1,0:T(8,128)(2,1)S(1)}) custom-call(bf16[16,16384]{1,0:T(8,128)(2,1)S(1)} %copy-done, bf16[4,16,2048]{2,1,0:T(8,128)(2,1)S(1)} %bitcast.13, bf16[2,128,1024]{2,1,0:T(8,128)(2,1)S(1)} %bitcast.11, bf16[2,128,1024]{2,1,0:T(8,128)(2,1)S(1)} %bitcast.12), custom_call_target="tpu_custom_call" | custom-call | flops 6442450944 | bytes 8388608 | tf_op jit(solution)/shard_map/pallas_call | solution.py:384
  141.8 1.6 %bitcast_convert_fusion = (f32[1,2,128,1024]{3,2,1,0:T(8,128)}, f32[1,2,128,1024]{3,2,1,0:T(8,128)}) fusion(bf16[2,128,1024]{2,1,0:T(8,128)(2,1)S(1)} %get-tuple-element.7, bf16[2,128,1024]{2,1,0:T(8,128)(2,1)S(1)} %get-tuple-element.6), kind=kLoop, calls=%fused_computation | loop fusion | flops 524288 | bytes 3145728 | tf_op jit(solution)/shard_map/convert_element_type | solution.py:425
  143.4 0.8 copy.8
Async XLA Ops:
  0.6 1.0 copy-start
  1.7 1.0 copy-start.1
  2.7 1.0 copy-start.2
  3.8 0.9 copy-start.3

commit v2 on v1

v2 whole, which is shorter than its diff:
```python
import functools

import jax
import jax.numpy as jnp
from jax import lax
from jax.experimental import pallas as pl
from jax.experimental.pallas import tpu as pltpu
from jax.sharding import PartitionSpec as P

MESH = pl.DeviceIdType.MESH
X, Y, Z, CORES = 4, 8, 8, 2
F = Y * CORES
T = Z // 2
PIECE = 128
BLOCK = 1024
HALF = BLOCK // 2
ROWS = 16
SLOT = F * ROWS
TILE = 256


def mod(value, size):
    return lax.rem(value + 2 * size, size)


def scaled(index, size):
    return pl.multiple_of(index * size, size)


def kernel(
    factor,
    a_ref, c_ref, lr_ref, rr_ref,
    left_ref, right_ref, upd_ref,
    stage, a_buf, c_buf, g_buf, r_buf, l_buf, at_buf, t_buf, relay, near, gt_buf, lift_buf,
    right_acc, lift_acc, o_buf,
    local_sem, swap_send, swap_recv,
    a_send, a_recv, c_send, c_recv, sib_send, sib_recv,
    z_send, z_recv, t_send, t_recv, g_send, g_recv, r_send, r_recv, o_send, o_recv,
):
    m = lax.axis_index("dp")
    f = lax.axis_index("fsdp")
    t = lax.axis_index("tensor")
    zl, x = lax.div(m, X), lax.rem(m, X)
    y, core = lax.div(f, CORES), lax.rem(f, CORES)
    z = 2 * t + zl
    other = 1 - zl

    def on_x(step):
        return (zl * X + mod(x + step, X), f, t)

    def on_y(step):
        return (m, mod(y + step, Y) * CORES + core, t)

    def on_z(step):
        there = mod(z + step, Z)
        return (lax.rem(there, 2) * X + x, f, lax.div(there, 2))

    def slot_of(there):
        return lax.rem(there, 2) * T + lax.div(there, 2)

    sibling = (m, y * CORES + 1 - core, t)
    partner = (other * X + x, f, t)
    sign = (1, -1)
    slot = slot_of(z)
    my_rows = scaled(f, ROWS)

    started = []

    def put(src, dst, send, recv, device):
        copy = pltpu.make_async_remote_copy(
            src_ref=src, dst_ref=dst, send_sem=send, recv_sem=recv,
            device_id=device, device_id_type=MESH,
        )
        copy.start()
        started.append(copy)

    def arrived(dst, recv):
        pltpu.make_async_remote_copy(
            src_ref=dst, dst_ref=dst, send_sem=recv, recv_sem=recv,
            device_id=sibling, device_id_type=MESH,
        ).wait_recv()

    barrier = pltpu.get_barrier_semaphore()

    def greet(d, carry):
        pl.semaphore_signal(barrier, inc=1, device_id=(m, mod(f + d, F), t), device_id_type=MESH)
        return carry

    for device in (on_z(1), on_z(-1), on_x(1), on_x(-1)):
        pl.semaphore_signal(barrier, inc=1, device_id=device, device_id_type=MESH)
    lax.fori_loop(1, F, greet, 0)

    local = [
        pltpu.make_async_copy(
            a_ref.at[:, pl.ds(scaled(f, BLOCK), BLOCK)],
            stage.at[pl.ds(my_rows, ROWS), :], local_sem.at[0]),
        pltpu.make_async_copy(
            c_ref.at[:, :, pl.ds(scaled(zl, BLOCK), BLOCK)],
            c_buf.at[pl.ds(zl * T, T), pl.ds(my_rows, ROWS), :], local_sem.at[1]),
        pltpu.make_async_copy(lr_ref.at[zl], l_buf.at[zl], local_sem.at[2]),
        pltpu.make_async_copy(rr_ref.at[zl], r_buf.at[zl, x], local_sem.at[3]),
    ]
    for copy in local:
        copy.start()
    pl.semaphore_wait(barrier, F - 1 + 4)

    def a_copy(part, d):
        to = mod(f + d, F)
        start = pl.multiple_of(to * BLOCK + part * HALF, HALF)
        return pltpu.make_async_remote_copy(
            src_ref=a_ref.at[:, pl.ds(start, HALF)],
            dst_ref=stage.at[pl.ds(my_rows, ROWS), pl.ds(part * HALF, HALF)],
            send_sem=a_send.at[part, d], recv_sem=a_recv.at[part, d],
            device_id=(m, to, t), device_id_type=MESH)

    def a_first(part):
        def body(d, carry):
            a_copy(part, d).start()
            return carry
        lax.fori_loop(1, F, body, 0)

    def a_event(part):
        def body(d, carry):
            rows = pl.ds(scaled(mod(f - d, F), ROWS), ROWS)
            arrived(stage.at[rows, pl.ds(part * HALF, HALF)], a_recv.at[part, d])
            return carry
        lax.fori_loop(1, F, body, 0)

    def a_drain(part):
        def body(d, carry):
            a_copy(part, d).wait_send()
            return carry
        lax.fori_loop(1, F, body, 0)

    def a_strips(part):
        for i in range(part * X, part * X + X):
            a_buf[i, slot] = stage[:, i * PIECE:(i + 1) * PIECE]

    def c_chunk(half, owner):
        return c_buf.at[pl.ds(half * T, T), pl.ds(scaled(owner, ROWS), ROWS), :]

    def c_share(src, half, owner, way, step):
        put(src, c_chunk(half, owner), sib_send.at[half, way, step], sib_recv.at[half, way, step], sibling)

    def c_first(src, half):
        for way in (0, 1):
            put(src, c_chunk(half, f), c_send.at[way, half, 0], c_recv.at[way, half, 1], on_y(sign[way]))
        c_share(src, half, f, 0, 0)

    def c_event(step):
        for half in (0, 1):
            for way in (0, 1):
                if step == Y // 2 and way != half:
                    continue
                owner = mod(y - sign[way] * step, Y) * CORES + core
                chunk = c_chunk(half, owner)
                arrived(chunk, c_recv.at[way, half, step])
                if step < Y // 2 - 1 or (step == Y // 2 - 1 and way == half):
                    put(chunk, chunk, c_send.at[way, half, step], c_recv.at[way, half, step + 1],
                        on_y(sign[way]))
                c_share(chunk, half, owner, way, step)

    def c_rest():
        for step in range(Y // 2 + 1):
            for half in (0, 1):
                for way in (0, 1):
                    if (step == Y // 2 and way != half) or (step == 0 and way == 1):
                        continue
                    owner = mod(y - sign[way] * step, Y) * CORES + 1 - core
                    arrived(c_chunk(half, owner), sib_recv.at[half, way, step])

    target = (mod(x + 2, X), mod(x + 1, X), mod(x - 1, X), x)

    def strip(j):
        return (j // X) * X + target[j % X]

    def z_put(j, way, step, owner):
        ref = a_buf.at[strip(j), owner]
        put(ref, ref, z_send.at[way, j, step], z_recv.at[way, j, step + 1], on_z(sign[way]))

    def z_first(j):
        for way in (0, 1):
            z_put(j, way, 0, slot)

    def z_event(j, step):
        for way in (0, 1):
            if step == Z // 2 and way != j % 2:
                continue
            owner = slot_of(mod(z - sign[way] * step, Z))
            arrived(a_buf.at[strip(j), owner], z_recv.at[way, j, step])
            if step < Z // 2 - 1 or (step == Z // 2 - 1 and way == j % 2):
                z_put(j, way, step, owner)

    def x_first(src_of, dst_of, send, recv, half):
        for way in (0, 1):
            put(src_of, dst_of, send.at[way, half, 0], recv.at[way, half, 1], on_x(sign[way]))

    def x_ring(ref_of, send, recv, step):
        for half in (0, 1):
            for way in (0, 1):
                if step == X // 2 and way != half:
                    continue
                ref = ref_of(half, mod(x - sign[way] * step, X))
                arrived(ref, recv.at[way, half, step])
                if step < X // 2 - 1 or (step == X // 2 - 1 and way == half):
                    put(ref, ref, send.at[way, half, step], recv.at[way, half, step + 1], on_x(sign[way]))

    def r_chunk(half, owner):
        return r_buf.at[half, owner]

    def r_first(src, half):
        x_first(src, r_chunk(half, x), r_send, r_recv, half)

    def r_event(step):
        x_ring(r_chunk, r_send, r_recv, step)

    def g_rows(h, owner):
        return pl.ds(pl.multiple_of((h * X + owner) * PIECE, PIECE), PIECE)

    def side(q):
        return pl.ds(q * HALF, HALF)

    def g_chunk(h):
        return lambda q, owner: g_buf.at[g_rows(h, owner), side(q)]

    def g_first(h, q):
        ref = g_chunk(h)(q, x)
        x_first(ref, ref, g_send.at[h], g_recv.at[h], q)

    def g_event(h, step):
        x_ring(g_chunk(h), g_send.at[h], g_recv.at[h], step)

    def columns(n):
        return pl.ds(pl.multiple_of(n * TILE, TILE), TILE)

    def turn(j):
        for k in range(Z):
            at_buf[j % X, :, pl.ds(k * SLOT, SLOT)] = a_buf[strip(j), k].T

    def multiply(j, q):
        h, part = j // X, j % X

        def body(n, carry):
            cols = columns(n)
            value = jnp.dot(
                at_buf[part], c_buf[:, :, cols].reshape(Z * SLOT, TILE),
                preferred_element_type=jnp.float32,
            ) * factor
            if (part, q) in ((1, 0), (2, 1)):
                value = value + relay[h, :, cols].astype(jnp.float32)
            if part == 3:
                value = value + near[h, 0, :, cols].astype(jnp.float32) + near[h, 1, :, cols].astype(jnp.float32)
                g_buf[g_rows(h, x), cols] = value.astype(jnp.bfloat16)
            else:
                t_buf[h, part, :, cols] = value.astype(jnp.bfloat16)
            return carry

        lax.fori_loop(q * 2, q * 2 + 2, body, 0)

    def t_wait(j, q):
        h, part = j // X, j % X
        if (part, q) in ((1, 0), (2, 1)):
            arrived(relay.at[h, :, side(q)], t_recv.at[h, 0, q])
        if part == 3:
            arrived(near.at[h, 0, :, side(q)], t_recv.at[h, 1, q])
            arrived(near.at[h, 1, :, side(q)], t_recv.at[h, 2, q])

    def t_put(j, q):
        h, part = j // X, j % X
        if part == 3:
            g_first(h, q)
            return
        way = (q, 0, 1)[part]
        dst = relay.at[h, :, side(q)] if part == 0 else near.at[h, way, :, side(q)]
        put(t_buf.at[h, part, :, side(q)], dst, t_send.at[h, part, q], t_recv.at[h, part, q], on_x(sign[way]))

    def term(j, q):
        t_wait(j, q)
        multiply(j, q)
        t_put(j, q)

    def own_rows():
        return jnp.concatenate([g_buf[g_rows(0, x), :], g_buf[g_rows(1, x), :]], axis=0)

    def keep(which, cols, value):
        value = value.astype(jnp.bfloat16)
        o_buf[which, 0, :, cols] = value[:PIECE]
        o_buf[which, 1, :, cols] = value[PIECE:]

    outs = (left_ref, right_ref, upd_ref)
    kept = []
    inverse = 1.0 / BLOCK

    def ship(which, q):
        put(o_buf.at[which, other, :, side(q)], outs[which].at[zl, :, side(q)],
            o_send.at[which, q], o_recv.at[which, q], partner)
        copy = pltpu.make_async_copy(
            o_buf.at[which, zl, :, side(q)], outs[which].at[zl, :, side(q)], local_sem.at[4 + which * 2 + q])
        copy.start()
        kept.append(copy)

    def over_tiles(first, last, tile):
        def body(n, carry):
            tile(columns(n))
            return carry
        lax.fori_loop(first, last, body, 0)

    def left_part(h):
        def tile(cols):
            keep(0, cols, inverse * lax.dot_general(
                own_rows(), g_buf[cols, :], (((1,), (1,)), ((), ())),
                preferred_element_type=jnp.float32))
        over_tiles(h * 2, h * 2 + 2, tile)
        ship(0, h)

    def turn_own(h):
        rows = pl.ds(h * HALF, HALF)
        for i in (0, 1):
            gt_buf[pl.ds(i * PIECE, PIECE), rows] = g_buf[rows, g_rows(i, x)].T

    def right_part(h):
        rows = pl.ds(h * HALF, HALF)
        turn_own(h)

        def tile(cols):
            value = inverse * jnp.dot(gt_buf[:, rows], g_buf[rows, cols], preferred_element_type=jnp.float32)
            if h == 0:
                right_acc[:, cols] = value
            else:
                keep(1, cols, right_acc[:, cols] + value)
        for q in (0, 1):
            over_tiles(q * 2, q * 2 + 2, tile)
            if h == 1:
                ship(1, q)

    def lift_part(h):
        rows = pl.ds(h * HALF, HALF)

        def tile(cols):
            roots = l_buf[:, :, rows].reshape(2 * PIECE, HALF)
            value = jnp.dot(roots, g_buf[rows, cols], preferred_element_type=jnp.float32)
            if h == 0:
                lift_acc[:, cols] = value
            else:
                lift_buf[:, cols] = (lift_acc[:, cols] + value).astype(jnp.bfloat16)
        over_tiles(0, 4, tile)

    def update_part():
        def tile(cols):
            keep(2, cols, jnp.dot(
                lift_buf[...], r_buf[:, :, :, cols].reshape(BLOCK, TILE),
                preferred_element_type=jnp.float32))
        for q in (0, 1):
            over_tiles(q * 2, q * 2 + 2, tile)
            ship(2, q)

    put(c_ref.at[:, :, pl.ds(scaled(other, BLOCK), BLOCK)], c_chunk(zl, f),
        swap_send.at[0], swap_recv.at[0], partner)
    a_first(0)
    put(rr_ref.at[other], r_chunk(zl, x), swap_send.at[1], swap_recv.at[1], partner)
    r_first(rr_ref.at[zl], zl)
    c_first(c_ref.at[:, :, pl.ds(scaled(zl, BLOCK), BLOCK)], zl)
    arrived(c_chunk(other, f), swap_recv.at[0])
    c_first(c_chunk(other, f), other)
    local[0].wait()
    a_event(0)
    a_strips(0)
    for j in range(4):
        z_first(j)
    arrived(r_chunk(other, x), swap_recv.at[1])
    r_first(r_chunk(other, x), other)
    for step in (1, 2, 3, 4):
        c_event(step)
        for j in range(4):
            z_event(j, step)
        if step == 2:
            a_first(1)
            put(lr_ref.at[other], l_buf.at[zl], swap_send.at[2], swap_recv.at[2], partner)
            r_event(1)
    local[1].wait()
    turn(0)
    c_rest()
    term(0, 0)
    term(0, 1)
    turn(1)
    term(1, 1)
    turn(2)
    term(2, 0)
    a_event(1)
    a_strips(1)
    z_first(4)
    z_first(5)
    term(1, 0)
    term(2, 1)
    turn(3)
    z_event(4, 1)
    z_first(6)
    z_event(4, 2)
    z_event(5, 1)
    z_first(7)
    term(3, 0)
    z_event(4, 3)
    term(3, 1)
    z_event(5, 2)
    z_event(6, 1)
    z_event(4, 4)
    turn(4)
    z_event(5, 3)
    z_event(6, 2)
    z_event(7, 1)
    term(4, 0)
    term(4, 1)
    z_event(5, 4)
    z_event(6, 3)
    z_event(7, 2)
    turn(5)
    g_event(0, 1)
    term(5, 1)
    z_event(6, 4)
    z_event(7, 3)
    turn(6)
    term(6, 0)
    term(5, 0)
    term(6, 1)
    z_event(7, 4)
    turn(7)
    term(7, 0)
    term(7, 1)
    g_event(0, 2)
    left_part(0)
    right_part(0)
    local[2].wait()
    arrived(l_buf.at[other], swap_recv.at[2])
    lift_part(0)
    g_event(1, 1)
    local[3].wait()
    r_event(2)
    g_event(1, 2)
    right_part(1)
    lift_part(1)
    update_part()
    left_part(1)

    a_drain(0)
    a_drain(1)
    for copy in started:
        copy.wait_send()
    for copy in kept:
        copy.wait()
    for which in range(3):
        for q in (0, 1):
            arrived(outs[which].at[other, :, side(q)], o_recv.at[which, q])


def on_device(activations, cotangent, left_root, right_root):
    tokens = cotangent.shape[0]
    factor = float(tokens * lax.axis_size("dp") * lax.axis_size("fsdp")) ** (-0.5)
    bf16 = jnp.bfloat16
    dma = pltpu.SemaphoreType.DMA
    anywhere = pl.BlockSpec(memory_space=pltpu.HBM)
    piece = jax.ShapeDtypeStruct((2, PIECE, BLOCK), bf16)
    left, right, update = pl.pallas_call(
        functools.partial(kernel, factor),
        out_shape=(piece, piece, piece),
        in_specs=[anywhere] * 4,
        out_specs=(anywhere,) * 3,
        scratch_shapes=[
            pltpu.VMEM((SLOT, BLOCK), bf16),
            pltpu.VMEM((2 * X, Z, SLOT, PIECE), bf16),
            pltpu.VMEM((Z, SLOT, BLOCK), bf16),
            pltpu.VMEM((BLOCK, BLOCK), bf16),
            pltpu.VMEM((2, X, PIECE, BLOCK), bf16),
            pltpu.VMEM((2, PIECE, BLOCK), bf16),
            pltpu.VMEM((X, PIECE, Z * SLOT), bf16),
            pltpu.VMEM((2, 3, PIECE, BLOCK), bf16),
            pltpu.VMEM((2, PIECE, BLOCK), bf16),
            pltpu.VMEM((2, 2, PIECE, BLOCK), bf16),
            pltpu.VMEM((2 * PIECE, BLOCK), bf16),
            pltpu.VMEM((2 * PIECE, BLOCK), bf16),
            pltpu.VMEM((2 * PIECE, BLOCK), jnp.float32),
            pltpu.VMEM((2 * PIECE, BLOCK), jnp.float32),
            pltpu.VMEM((3, 2, PIECE, BLOCK), bf16),
            dma((10,)), dma((3,)), dma((3,)),
            dma((2, F)), dma((2, F)),
            dma((2, 2, 5)), dma((2, 2, 5)), dma((2, 2, 5)), dma((2, 2, 5)),
            dma((2, 8, 5)), dma((2, 8, 5)),
            dma((2, 3, 2)), dma((2, 3, 2)),
            dma((2, 2, 2, 3)), dma((2, 2, 2, 3)),
            dma((2, 2, 3)), dma((2, 2, 3)),
            dma((3, 2)), dma((3, 2)),
        ],
        compiler_params=pltpu.CompilerParams(
            collective_id=0, has_side_effects=True, vmem_limit_bytes=62 * 1024 * 1024
        ),
        cost_estimate=pl.CostEstimate(
            flops=6 * 2**30, bytes_accessed=8 * 2**20, transcendentals=0),
    )(
        activations,
        cotangent.reshape(T, ROWS, 2 * BLOCK),
        left_root.reshape(2, PIECE, BLOCK),
        right_root.reshape(2, PIECE, BLOCK),
    )
    shape = left_root.shape
    return (
        left.reshape(shape).astype(jnp.float32),
        right.reshape(shape).astype(jnp.float32),
        update.reshape(shape),
    )


def solution(mesh):
    return jax.shard_map(
        on_device,
        mesh=mesh,
        in_specs=(
            P(("dp", "fsdp", "tensor"), None),
            P(("dp", "fsdp"), "tensor"),
            P("fsdp", "tensor", "dp", None),
            P("fsdp", "tensor", "dp", None),
        ),
        out_specs=(
            P("fsdp", "tensor", "dp", None),
            P("fsdp", "tensor", "dp", None),
            P("fsdp", "tensor", "dp", None),
        ),
        check_vma=False,
    )
```

time: 144 us -> 119 us (0.83)
  the two profiles are of different devices: /device:TPU:2 before, /device:TPU:28 now
where the time goes in v2:
time: 119 us
  Pallas kernels  115 us (97%)
  other arithmetic  2.82 us (2%)
    pallas_call x1, Pallas kernels, on_device(): pl.pallas_call(functools.partial(kernel, factor), out_shape=(piece, piece...  115 us
    convert_element_type x1, other arithmetic, on_device(): right.reshape(shape).astype(jnp.float32)  2.82 us

profile of v2, /device:TPU:28, one launch (start us, length us, event | category | flops | bytes accessed | tf_op | source)
XLA Modules:
  0.0 119.3 jit_solution(224453660829966418)
XLA Ops:
  0.6 115.0 %shard_map.67 = (bf16[2,128,1024]{2,1,0:T(8,128)(2,1)}, bf16[2,128,1024]{2,1,0:T(8,128)(2,1)}, bf16[2,128,1024]{2,1,0:T(8,128)(2,1)}) custom-call(bf16[16,16384]{1,0:T(8,128)(2,1)} %a_ref.1, bf16[4,16,2048]{2,1,0:T(8,128)(2,1)} %bitcast.13, bf16[2,128,1024]{2,1,0:T(8,128)(2,1)} %bitcast.11, bf16[2,128,1024]{2,1,0:T(8,128)(2,1)} %bitcast.12), custom_call_target="tpu_custom_call" | custom-call | flops 6442450944 | bytes 8388608 | tf_op jit(solution)/shard_map/pallas_call | solution.py:462
  115.7 0.0 copy-start
  115.7 2.8 %bitcast_convert_fusion = (f32[1,2,128,1024]{3,2,1,0:T(8,128)}, f32[1,2,128,1024]{3,2,1,0:T(8,128)}) fusion(bf16[2,128,1024]{2,1,0:T(8,128)(2,1)} %get-tuple-element.7, bf16[2,128,1024]{2,1,0:T(8,128)(2,1)} %get-tuple-element.6), kind=kLoop, calls=%fused_computation | loop fusion | flops 524288 | bytes 3145728 | tf_op jit(solution)/shard_map/convert_element_type | solution.py:506
  118.5 0.0 copy-done
  118.5 0.8 copy.8
Async XLA Ops:
  115.7 2.8 %copy-start = (bf16[2,128,1024]{2,1,0:T(8,128)(2,1)S(1)}, bf16[2,128,1024]{2,1,0:T(8,128)(2,1)}, u32[]{:S(2)}) copy-start(bf16[2,128,1024]{2,1,0:T(8,128)(2,1)} %get-tuple-element.8) | copy-start | bytes 1572868

commit v3 on v2

--- a/solution.py
+++ b/solution.py
@@ -30,7 +30,7 @@
 def kernel(
     factor,
     a_ref, c_ref, lr_ref, rr_ref,
-    left_ref, right_ref, upd_ref,
+    out_ref,
     stage, a_buf, c_buf, g_buf, r_buf, l_buf, at_buf, t_buf, relay, near, gt_buf, lift_buf,
     right_acc, lift_acc, o_buf,
     local_sem, swap_send, swap_recv,
@@ -147,18 +147,17 @@
             put(src, c_chunk(half, f), c_send.at[way, half, 0], c_recv.at[way, half, 1], on_y(sign[way]))
         c_share(src, half, f, 0, 0)
 
-    def c_event(step):
-        for half in (0, 1):
-            for way in (0, 1):
-                if step == Y // 2 and way != half:
-                    continue
-                owner = mod(y - sign[way] * step, Y) * CORES + core
-                chunk = c_chunk(half, owner)
-                arrived(chunk, c_recv.at[way, half, step])
-                if step < Y // 2 - 1 or (step == Y // 2 - 1 and way == half):
-                    put(chunk, chunk, c_send.at[way, half, step], c_recv.at[way, half, step + 1],
-                        on_y(sign[way]))
-                c_share(chunk, half, owner, way, step)
+    def c_event(step, half):
+        for way in (0, 1):
+            if step == Y // 2 and way != half:
+                continue
+            owner = mod(y - sign[way] * step, Y) * CORES + core
+            chunk = c_chunk(half, owner)
+            arrived(chunk, c_recv.at[way, half, step])
+            if step < Y // 2 - 1 or (step == Y // 2 - 1 and way == half):
+                put(chunk, chunk, c_send.at[way, half, step], c_recv.at[way, half, step + 1],
+                    on_y(sign[way]))
+            c_share(chunk, half, owner, way, step)
 
     def c_rest():
         for step in range(Y // 2 + 1):
@@ -196,8 +195,9 @@
             put(src_of, dst_of, send.at[way, half, 0], recv.at[way, half, 1], on_x(sign[way]))
 
     def x_ring(ref_of, send, recv, step):
-        for half in (0, 1):
+        for turned in (0, 1):
             for way in (0, 1):
+                half = (way + turned) % 2
                 if step == X // 2 and way != half:
                     continue
                 ref = ref_of(half, mod(x - sign[way] * step, X))
@@ -223,9 +223,12 @@
     def g_chunk(h):
         return lambda q, owner: g_buf.at[g_rows(h, owner), side(q)]
 
-    def g_first(h, q):
-        ref = g_chunk(h)(q, x)
-        x_first(ref, ref, g_send.at[h], g_recv.at[h], q)
+    def g_first(h):
+        for q in (0, 1):
+            for way in (0, 1):
+                half = (way + q) % 2
+                ref = g_chunk(h)(half, x)
+                put(ref, ref, g_send.at[h, way, half, 0], g_recv.at[h, way, half, 1], on_x(sign[way]))
 
     def g_event(h, step):
         x_ring(g_chunk(h), g_send.at[h], g_recv.at[h], step)
@@ -268,7 +271,8 @@
     def t_put(j, q):
         h, part = j // X, j % X
         if part == 3:
-            g_first(h, q)
+            if q == 1:
+                g_first(h)
             return
         way = (q, 0, 1)[part]
         dst = relay.at[h, :, side(q)] if part == 0 else near.at[h, way, :, side(q)]
@@ -287,15 +291,14 @@
         o_buf[which, 0, :, cols] = value[:PIECE]
         o_buf[which, 1, :, cols] = value[PIECE:]
 
-    outs = (left_ref, right_ref, upd_ref)
     kept = []
     inverse = 1.0 / BLOCK
 
-    def ship(which, q):
-        put(o_buf.at[which, other, :, side(q)], outs[which].at[zl, :, side(q)],
-            o_send.at[which, q], o_recv.at[which, q], partner)
+    def ship(which, cols, i):
+        put(o_buf.at[which, other, :, cols], out_ref.at[which, zl, :, cols],
+            o_send.at[which, i], o_recv.at[which, i], partner)
         copy = pltpu.make_async_copy(
-            o_buf.at[which, zl, :, side(q)], outs[which].at[zl, :, side(q)], local_sem.at[4 + which * 2 + q])
+            o_buf.at[which, zl, :, cols], out_ref.at[which, zl, :, cols], local_sem.at[4 + which * 5 + i])
         copy.start()
         kept.append(copy)
 
@@ -305,13 +308,19 @@
             return carry
         lax.fori_loop(first, last, body, 0)
 
-    def left_part(h):
-        def tile(cols):
-            keep(0, cols, inverse * lax.dot_general(
-                own_rows(), g_buf[cols, :], (((1,), (1,)), ((), ())),
-                preferred_element_type=jnp.float32))
-        over_tiles(h * 2, h * 2 + 2, tile)
-        ship(0, h)
+    def left_tile(cols):
+        keep(0, cols, inverse * lax.dot_general(
+            own_rows(), g_buf[cols, :], (((1,), (1,)), ((), ())),
+            preferred_element_type=jnp.float32))
+
+    def left_part():
+        over_tiles(0, 2, left_tile)
+        ship(0, side(0), 0)
+
+    def left_piece(i):
+        cols = g_rows(1, target[i])
+        left_tile(cols)
+        ship(0, cols, 1 + i)
 
     def turn_own(h):
         rows = pl.ds(h * HALF, HALF)
@@ -331,7 +340,7 @@
         for q in (0, 1):
             over_tiles(q * 2, q * 2 + 2, tile)
             if h == 1:
-                ship(1, q)
+                ship(1, side(q), q)
 
     def lift_part(h):
         rows = pl.ds(h * HALF, HALF)
@@ -352,15 +361,15 @@
                 preferred_element_type=jnp.float32))
         for q in (0, 1):
             over_tiles(q * 2, q * 2 + 2, tile)
-            ship(2, q)
+            ship(2, side(q), q)
 
     put(c_ref.at[:, :, pl.ds(scaled(other, BLOCK), BLOCK)], c_chunk(zl, f),
         swap_send.at[0], swap_recv.at[0], partner)
     a_first(0)
     put(rr_ref.at[other], r_chunk(zl, x), swap_send.at[1], swap_recv.at[1], partner)
     r_first(rr_ref.at[zl], zl)
+    arrived(c_chunk(other, f), swap_recv.at[0])
     c_first(c_ref.at[:, :, pl.ds(scaled(zl, BLOCK), BLOCK)], zl)
-    arrived(c_chunk(other, f), swap_recv.at[0])
     c_first(c_chunk(other, f), other)
     local[0].wait()
     a_event(0)
@@ -369,57 +378,76 @@
         z_first(j)
     arrived(r_chunk(other, x), swap_recv.at[1])
     r_first(r_chunk(other, x), other)
-    for step in (1, 2, 3, 4):
-        c_event(step)
-        for j in range(4):
-            z_event(j, step)
-        if step == 2:
-            a_first(1)
-            put(lr_ref.at[other], l_buf.at[zl], swap_send.at[2], swap_recv.at[2], partner)
-            r_event(1)
-    local[1].wait()
-    turn(0)
-    c_rest()
-    term(0, 0)
-    term(0, 1)
-    turn(1)
-    term(1, 1)
-    turn(2)
-    term(2, 0)
+    c_event(1, 0)
+    c_event(1, 1)
+    z_event(0, 1)
+    z_event(1, 1)
+    c_event(2, 0)
+    z_event(2, 1)
+    z_event(3, 1)
+    c_event(2, 1)
+    z_event(0, 2)
+    z_event(1, 2)
+    r_event(1)
+    c_event(3, 0)
+    a_first(1)
+    z_event(2, 2)
+    z_event(3, 2)
+    c_event(3, 1)
+    z_event(0, 3)
+    z_event(1, 3)
+    put(lr_ref.at[other], l_buf.at[zl], swap_send.at[2], swap_recv.at[2], partner)
+    z_event(2, 3)
+    z_event(3, 3)
     a_event(1)
     a_strips(1)
     z_first(4)
     z_first(5)
-    term(1, 0)
-    term(2, 1)
-    turn(3)
+    z_first(6)
+    local[1].wait()
+    c_event(4, 0)
+    c_event(4, 1)
+    z_event(0, 4)
+    turn(0)
+    z_event(1, 4)
+    turn(1)
+    c_rest()
+    term(0, 0)
+    term(0, 1)
     z_event(4, 1)
-    z_first(6)
-    z_event(4, 2)
     z_event(5, 1)
     z_first(7)
+    term(1, 1)
+    z_event(2, 4)
+    turn(2)
+    term(2, 0)
+    z_event(3, 4)
+    turn(3)
+    z_event(6, 1)
+    z_event(4, 2)
+    z_event(5, 2)
+    term(1, 0)
+    z_event(7, 1)
+    term(2, 1)
+    z_event(4, 3)
+    z_event(6, 2)
+    z_event(5, 3)
     term(3, 0)
-    z_event(4, 3)
     term(3, 1)
-    z_event(5, 2)
-    z_event(6, 1)
+    z_event(7, 2)
     z_event(4, 4)
     turn(4)
-    z_event(5, 3)
-    z_event(6, 2)
-    z_event(7, 1)
     term(4, 0)
     term(4, 1)
     z_event(5, 4)
+    turn(5)
+    term(5, 1)
     z_event(6, 3)
-    z_event(7, 2)
-    turn(5)
-    g_event(0, 1)
-    term(5, 1)
+    z_event(7, 3)
     z_event(6, 4)
-    z_event(7, 3)
     turn(6)
     term(6, 0)
+    g_event(0, 1)
     term(5, 0)
     term(6, 1)
     z_event(7, 4)
@@ -427,19 +455,22 @@
     term(7, 0)
     term(7, 1)
     g_event(0, 2)
-    left_part(0)
+    left_part()
     right_part(0)
     local[2].wait()
     arrived(l_buf.at[other], swap_recv.at[2])
     lift_part(0)
+    left_piece(3)
     g_event(1, 1)
+    left_piece(2)
+    left_piece(1)
     local[3].wait()
     r_event(2)
     g_event(1, 2)
     right_part(1)
     lift_part(1)
     update_part()
-    left_part(1)
+    left_piece(0)
 
     a_drain(0)
     a_drain(1)
@@ -447,9 +478,12 @@
         copy.wait_send()
     for copy in kept:
         copy.wait()
-    for which in range(3):
+    for which in (1, 2):
         for q in (0, 1):
-            arrived(outs[which].at[other, :, side(q)], o_recv.at[which, q])
+            arrived(out_ref.at[which, other, :, side(q)], o_recv.at[which, q])
+    arrived(out_ref.at[0, other, :, side(0)], o_recv.at[0, 0])
+    for i in range(X):
+        arrived(out_ref.at[0, other, :, g_rows(1, target[i])], o_recv.at[0, 1 + i])
 
 
 def on_device(activations, cotangent, left_root, right_root):
@@ -458,12 +492,11 @@
     bf16 = jnp.bfloat16
     dma = pltpu.SemaphoreType.DMA
     anywhere = pl.BlockSpec(memory_space=pltpu.HBM)
-    piece = jax.ShapeDtypeStruct((2, PIECE, BLOCK), bf16)
-    left, right, update = pl.pallas_call(
+    out = pl.pallas_call(
         functools.partial(kernel, factor),
-        out_shape=(piece, piece, piece),
+        out_shape=jax.ShapeDtypeStruct((3, 2, PIECE, BLOCK), bf16),
         in_specs=[anywhere] * 4,
-        out_specs=(anywhere,) * 3,
+        out_specs=anywhere,
         scratch_shapes=[
             pltpu.VMEM((SLOT, BLOCK), bf16),
             pltpu.VMEM((2 * X, Z, SLOT, PIECE), bf16),
@@ -480,14 +513,14 @@
             pltpu.VMEM((2 * PIECE, BLOCK), jnp.float32),
             pltpu.VMEM((2 * PIECE, BLOCK), jnp.float32),
             pltpu.VMEM((3, 2, PIECE, BLOCK), bf16),
-            dma((10,)), dma((3,)), dma((3,)),
+            dma((20,)), dma((3,)), dma((3,)),
             dma((2, F)), dma((2, F)),
             dma((2, 2, 5)), dma((2, 2, 5)), dma((2, 2, 5)), dma((2, 2, 5)),
             dma((2, 8, 5)), dma((2, 8, 5)),
             dma((2, 3, 2)), dma((2, 3, 2)),
             dma((2, 2, 2, 3)), dma((2, 2, 2, 3)),
             dma((2, 2, 3)), dma((2, 2, 3)),
-            dma((3, 2)), dma((3, 2)),
+            dma((3, 5)), dma((3, 5)),
         ],
         compiler_params=pltpu.CompilerParams(
             collective_id=0, has_side_effects=True, vmem_limit_bytes=62 * 1024 * 1024
@@ -502,9 +535,9 @@
     )
     shape = left_root.shape
     return (
-        left.reshape(shape).astype(jnp.float32),
-        right.reshape(shape).astype(jnp.float32),
-        update.reshape(shape),
+        out[0].reshape(shape).astype(jnp.float32),
+        out[1].reshape(shape).astype(jnp.float32),
+        out[2].reshape(shape),
     )
 
 

time: 119 us -> 116 us (0.975)
  the two profiles are of different devices: /device:TPU:28 before, /device:TPU:1 now
where the time goes in v3:
time: 116 us; the launch traced here: 113 us
  Pallas kernels  110 us (95%)
  other arithmetic  2.96 us (3%)
    pallas_call x1, Pallas kernels, on_device(): pl.pallas_call(functools.partial(kernel, factor), out_shape=jax.ShapeDtyp...  110 us
    slice x1, other arithmetic, on_device(): out[2].reshape(shape)  2.96 us

profile of v3, /device:TPU:1, one launch (start us, length us, event | category | flops | bytes accessed | tf_op | source)
XLA Modules:
  0.0 113.3 jit_solution(7574279321268456910)
XLA Ops:
  0.6 109.7 %shard_map.67 = bf16[3,2,128,1024]{3,2,1,0:T(8,128)(2,1)} custom-call(bf16[16,16384]{1,0:T(8,128)(2,1)} %a_ref.1, bf16[4,16,2048]{2,1,0:T(8,128)(2,1)} %bitcast.5, bf16[2,128,1024]{2,1,0:T(8,128)(2,1)} %bitcast.3, bf16[2,128,1024]{2,1,0:T(8,128)(2,1)} %bitcast.4), custom_call_target="tpu_custom_call" | custom-call | flops 6442450944 | bytes 8388608 | tf_op jit(solution)/shard_map/pallas_call | solution.py:495
  110.3 3.0 %fusion = (bf16[1,2,128,1024]{3,2,1,0:T(8,128)(2,1)}, f32[1,2,128,1024]{3,2,1,0:T(8,128)}, f32[1,2,128,1024]{3,2,1,0:T(8,128)}) fusion(bf16[3,2,128,1024]{3,2,1,0:T(8,128)(2,1)} %shard_map.67), kind=kLoop, calls=%fused_computation.2 | loop fusion | flops 524288 | bytes 4194304 | tf_op jit(solution)/shard_map/slice | solution.py:540

commit v4 on v3

--- a/solution.py
+++ b/solution.py
@@ -523,16 +523,19 @@
             dma((3, 5)), dma((3, 5)),
         ],
         compiler_params=pltpu.CompilerParams(
-            collective_id=0, has_side_effects=True, vmem_limit_bytes=62 * 1024 * 1024
+            collective_id=0, has_side_effects=True, vmem_limit_bytes=40 * 1024 * 1024
         ),
         cost_estimate=pl.CostEstimate(
             flops=6 * 2**30, bytes_accessed=8 * 2**20, transcendentals=0),
-    )(
-        activations,
-        cotangent.reshape(T, ROWS, 2 * BLOCK),
-        left_root.reshape(2, PIECE, BLOCK),
-        right_root.reshape(2, PIECE, BLOCK),
-    )
+    )(*(
+        pltpu.with_memory_space_constraint(value, pltpu.HBM)
+        for value in (
+            activations,
+            cotangent.reshape(T, ROWS, 2 * BLOCK),
+            left_root.reshape(2, PIECE, BLOCK),
+            right_root.reshape(2, PIECE, BLOCK),
+        )
+    ))
     shape = left_root.shape
     return (
         out[0].reshape(shape).astype(jnp.float32),

time: 116 us -> 114 us (0.983)
  other arithmetic: 2.96 us -> 1.6 us
    slice x1, other arithmetic: 2.96 us -> 1.6 us  [on_device(): out[2].reshape(shape)]
where the time goes in v4:
time: 114 us; the launch traced here: 112 us
  Pallas kernels  110 us (96%)
  other arithmetic  1.6 us (1%)
    pallas_call x1, Pallas kernels, on_device(): pl.pallas_call(functools.partial(kernel, factor), out_shape=jax.ShapeDtyp...  110 us

profile of v4, /device:TPU:1, one launch (start us, length us, event | category | flops | bytes accessed | tf_op | source)
XLA Modules:
  0.0 111.9 jit_solution(5142299786065669431)
XLA Ops:
  0.6 109.7 %shard_map.67 = bf16[3,2,128,1024]{3,2,1,0:T(8,128)(2,1)S(1)} custom-call(bf16[16,16384]{1,0:T(8,128)(2,1)} %a_ref.1, bf16[4,16,2048]{2,1,0:T(8,128)(2,1)} %bitcast.5, bf16[2,128,1024]{2,1,0:T(8,128)(2,1)} %bitcast.3, bf16[2,128,1024]{2,1,0:T(8,128)(2,1)} %bitcast.4), custom_call_target="tpu_custom_call" | custom-call | flops 6442450944 | bytes 8388608 | tf_op jit(solution)/shard_map/pallas_call | solution.py:495
  110.3 1.6 %fusion = (bf16[1,2,128,1024]{3,2,1,0:T(8,128)(2,1)}, f32[1,2,128,1024]{3,2,1,0:T(8,128)}, f32[1,2,128,1024]{3,2,1,0:T(8,128)}) fusion(bf16[3,2,128,1024]{3,2,1,0:T(8,128)(2,1)S(1)} %shard_map.67), kind=kLoop, calls=%fused_computation.2 | loop fusion | flops 524288 | bytes 4194304 | tf_op jit(solution)/shard_map/slice | solution.py:543

commit v5 on v4

--- a/solution.py
+++ b/solution.py
@@ -432,13 +432,13 @@
     z_event(4, 3)
     z_event(6, 2)
     z_event(5, 3)
-    term(3, 0)
-    term(3, 1)
     z_event(7, 2)
     z_event(4, 4)
     turn(4)
     term(4, 0)
     term(4, 1)
+    term(3, 0)
+    term(3, 1)
     z_event(5, 4)
     turn(5)
     term(5, 1)

time: 114 us -> 118 us (1.035); the launches traced: 112 us -> 117 us
  Pallas kernels: 110 us -> 115 us
    pallas_call x1, Pallas kernels: 110 us -> 115 us  [on_device(): pl.pallas_call(functools.partial(kernel, factor), out_shape=jax.ShapeDtyp...]
where the time goes in v5:
time: 118 us; the launch traced here: 117 us
  Pallas kernels  115 us (97%)
  other arithmetic  1.6 us (1%)
    pallas_call x1, Pallas kernels, on_device(): pl.pallas_call(functools.partial(kernel, factor), out_shape=jax.ShapeDtyp...  115 us

profile of v5, /device:TPU:1, one launch (start us, length us, event | category | flops | bytes accessed | tf_op | source)
XLA Modules:
  0.0 117.2 jit_solution(3206359897197841712)
XLA Ops:
  0.6 114.9 %shard_map.67 = bf16[3,2,128,1024]{3,2,1,0:T(8,128)(2,1)S(1)} custom-call(bf16[16,16384]{1,0:T(8,128)(2,1)} %a_ref.1, bf16[4,16,2048]{2,1,0:T(8,128)(2,1)} %bitcast.5, bf16[2,128,1024]{2,1,0:T(8,128)(2,1)} %bitcast.3, bf16[2,128,1024]{2,1,0:T(8,128)(2,1)} %bitcast.4), custom_call_target="tpu_custom_call" | custom-call | flops 6442450944 | bytes 8388608 | tf_op jit(solution)/shard_map/pallas_call | solution.py:495
  115.6 1.6 %fusion = (bf16[1,2,128,1024]{3,2,1,0:T(8,128)(2,1)}, f32[1,2,128,1024]{3,2,1,0:T(8,128)}, f32[1,2,128,1024]{3,2,1,0:T(8,128)}) fusion(bf16[3,2,128,1024]{3,2,1,0:T(8,128)(2,1)S(1)} %shard_map.67), kind=kLoop, calls=%fused_computation.2 | loop fusion | flops 524288 | bytes 4194304 | tf_op jit(solution)/shard_map/slice | solution.py:543
